TPU v7x, 256 devices: a whole 4x4x8 slice. The times are simulated.
256 devices in a mesh: gx: 8 (over x, z_lo), gy: 32 (over y, z_hi, core).
Axes of the slice: x: 4, y: 4, z: 8 (z_hi: 4, z_lo: 2; z = z_hi * 2 + z_lo), core: 2. Of those that a mesh axis runs over, the one named last changes fastest.
Arguments:
- coeff: float32 [2, 64, 8, 32, 4096], P(None, None, 'gx', 'gy'), may hold values from -6 to 6
- phase_x: float32 [4, 2, 64, 8], replicated, may hold values from -3.140625 to 3.140625
- phase_y: float32 [4, 2, 64, 32], replicated, may hold values from -3.140625 to 3.140625
- phase_q: float32 [4, 2, 64, 4096], replicated, may hold values from -3.140625 to 3.140625
- interp: float32 [4, 64, 64], replicated, may hold values from -0.07 to 0.57
Outputs:
- result: float32 [2, 64, 8, 32, 4096], P(None, None, 'gx', 'gy')
All inputs are finite; a program needn't handle non-finite values.
Results may differ from a plain program's by a relative error of at most 0.00011.
Values sent between devices are 32-bit elements; how exact they have to be, the bound alone decides.
A program may use at most 128 MiB of HBM per device.

v0:
```python
import jax
import jax.numpy as jnp
from jax import lax
from jax.sharding import PartitionSpec as P

LEVELS = 4


def partner(x, axis, distance):
    return lax.ppermute(x, axis, [(i, i ^ 1 << distance) for i in range(lax.axis_size(axis))])


def rotate_in(values, angle):
    cosine = jnp.cos(angle)
    sine_part = jnp.sin(angle)
    return jnp.stack(
        [values[0] * cosine + values[1] * sine_part, values[1] * cosine - values[0] * sine_part]
    )


def rotate_out(values, angle):
    cosine = jnp.cos(angle)
    sine_part = jnp.sin(angle)
    return jnp.stack(
        [values[0] * cosine - values[1] * sine_part, values[0] * sine_part + values[1] * cosine]
    )


def own_angles(part_x, part_y, part_q, index_x, index_y):
    own_x = lax.dynamic_index_in_dim(part_x, index_x, 1, keepdims=True)
    own_y = lax.dynamic_index_in_dim(part_y, index_y, 1, keepdims=True)
    return own_x[:, :, None, None] + own_y[:, None, :, None] + part_q[:, None, None, :]


def per_device(coeff, phase_x, phase_y, phase_q, interp):
    count_x = lax.axis_size("gx")
    count_y = lax.axis_size("gy")
    bits_x = count_x.bit_length() - 1
    bits_y = count_y.bit_length() - 1
    index_x = lax.axis_index("gx")
    index_y = lax.axis_index("gy")
    coeffs = coeff
    for step_no in range(LEVELS):
        bit_x = (bits_x - 1 - step_no) % bits_x
        bit_y = (bits_y - 1 - step_no) % bits_y
        angle_in = own_angles(
            phase_x[step_no, 0], phase_y[step_no, 0], phase_q[step_no, 0], index_x, index_y
        )
        angle_out = own_angles(
            phase_x[step_no, 1], phase_y[step_no, 1], phase_q[step_no, 1], index_x, index_y
        )
        turned = rotate_in(coeffs, angle_in)
        summed = turned + partner(turned, "gx", bit_x)
        summed = summed + partner(summed, "gy", bit_y)
        block_no = 2 * (index_x >> bit_x & 1) + (index_y >> bit_y & 1)
        blocks = lax.dynamic_index_in_dim(interp, block_no, 0, keepdims=False)
        mapped = jnp.einsum("tk,rkabq->rtabq", blocks, summed, precision=lax.Precision.HIGHEST)
        coeffs = rotate_out(mapped, angle_out)
    return coeffs


def solution(mesh):
    placed = (P(None, None, "gx", "gy", None), P(), P(), P(), P())
    return jax.shard_map(
        per_device,
        mesh=mesh,
        in_specs=placed,
        out_specs=P(None, None, "gx", "gy", None),
        check_vma=False,
    )
```

profile of v0, /device:TPU:8, one launch (start us, length us, event | category | flops | bytes accessed | tf_op | source)
XLA Modules:
  0.0 543.9 jit_solution(10715701121161050746)
XLA Ops:
  0.0 0.0 copy-start
  0.0 0.8 fusion.58
  0.8 0.8 fusion.57
  1.7 1.7 fusion.56
  3.4 6.8 %multiply_add_fusion.7 = (f32[1,64,1,1,4096]{4,1,3,2,0:T(8,128)S(1)}, f32[1,64,1,1,4096]{4,1,3,2,0:T(8,128)S(1)}) fusion(f32[1,64,1,1,4096]{4,3,2,1,0:T(1,128)S(1)} %get-tuple-element.19, f32[1,64,1,1,4096]{4,3,2,1,0:T(1,128)S(1)} %get-tuple-element.18, f32[4,2,64,4096]{3,2,1,0:T(8,128)} %param.8, f32[64]{0:T(128)S(1)} %fusion.37), kind=kLoop, calls=%fused_computation.40 | loop fusion | flops 1835008 | bytes 5243136 | tf_op jit(solution)/shard_map/add | solution.py:17
  10.2 0.2 pad_maximum_fusion
  10.4 3.1 collective-permute-start
  13.5 45.8 %collective-permute-done = f32[2,64,1,1,4096]{4,1,3,2,0:T(8,128)S(1)} collective-permute-done((f32[2,64,1,1,4096]{4,1,3,2,0:T(8,128)S(1)}, f32[2,64,1,1,4096]{4,1,3,2,0:T(8,128)S(1)}, u32[]{:S(2)}, u32[]{:S(2)}) %collective-permute-start) | collective-permute-done | bytes 2097184 | tf_op jit(solution)/shard_map/ppermute | solution.py:10
  59.4 0.2 fusion.55
  59.6 2.4 collective-permute-start.1
  62.0 45.8 %collective-permute-done.1 = f32[2,64,1,1,4096]{4,1,3,2,0:T(8,128)} collective-permute-done((f32[2,64,1,1,4096]{4,1,3,2,0:T(8,128)S(1)}, f32[2,64,1,1,4096]{4,1,3,2,0:T(8,128)}, u32[]{:S(2)}, u32[]{:S(2)}) %collective-permute-start.1) | collective-permute-done | bytes 2097184 | tf_op jit(solution)/shard_map/ppermute | solution.py:10
  107.8 0.0 copy-done
  107.8 3.7 convolution_bitcast_fusion.3
  111.5 9.3 %multiply_add_fusion.5 = (f32[1,64,1,1,4096]{4,1,0,3,2:T(8,128)S(1)}, f32[1,64,1,1,4096]{4,1,0,3,2:T(8,128)S(1)}, f32[1,64,1,1,4096]{4,1,0,3,2:T(8,128)S(1)}) fusion(f32[4,2,64,4096]{3,2,1,0:T(8,128)} %param.8, f32[64]{0:T(128)S(1)} %get-tuple-element.37, f32[2,64,1,1,4096]{4,1,0,3,2:T(8,128)S(1)} %convolution_bitcast_fusion.3, f32[64]{0:T(128)S(1)} %get-tuple-element.36), kind=kLoop, calls=%fused_computation.36 | loop fusion | flops 2883584 | bytes 7340544 | tf_op jit(solution)/shard_map/add | solution.py:17
  120.8 5.0 multiply_subtract_fusion.5
  125.8 0.2 pad_maximum_fusion.1
  126.0 1.6 collective-permute-start.2
  127.6 44.1 %collective-permute-done.2 = f32[2,64,1,1,4096]{4,1,0,3,2:T(8,128)S(1)} collective-permute-done((f32[2,64,1,1,4096]{4,1,0,3,2:T(8,128)S(1)}, f32[2,64,1,1,4096]{4,1,0,3,2:T(8,128)S(1)}, u32[]{:S(2)}, u32[]{:S(2)}) %collective-permute-start.2) | collective-permute-done | bytes 2097184 | tf_op jit(solution)/shard_map/ppermute | solution.py:10
  171.7 0.2 fusion.54
  171.9 0.8 collective-permute-start.3
  172.8 44.2 %collective-permute-done.3 = f32[2,64,1,1,4096]{4,1,0,3,2:T(8,128)} collective-permute-done((f32[2,64,1,1,4096]{4,1,0,3,2:T(8,128)S(1)}, f32[2,64,1,1,4096]{4,1,0,3,2:T(8,128)}, u32[]{:S(2)}, u32[]{:S(2)}) %collective-permute-start.3) | collective-permute-done | bytes 2097184 | tf_op jit(solution)/shard_map/ppermute | solution.py:10
  217.0 3.7 convolution_bitcast_fusion.2
  220.7 9.3 %multiply_add_fusion.3 = (f32[1,64,1,1,4096]{4,1,0,3,2:T(8,128)S(1)}, f32[1,64,1,1,4096]{4,1,0,3,2:T(8,128)S(1)}, f32[1,64,1,1,4096]{4,1,0,3,2:T(8,128)S(1)}) fusion(f32[4,2,64,4096]{3,2,1,0:T(8,128)} %param.8, f32[64]{0:T(128)S(1)} %get-tuple-element.39, f32[2,64,1,1,4096]{4,1,0,3,2:T(8,128)S(1)} %convolution_bitcast_fusion.2, f32[64]{0:T(128)S(1)} %get-tuple-element.38), kind=kLoop, calls=%fused_computation.32 | loop fusion | flops 2883584 | bytes 7340544 | tf_op jit(solution)/shard_map/add | solution.py:17
  229.9 5.0 multiply_subtract_fusion.3
  235.0 0.2 pad_maximum_fusion.2
  235.2 2.0 collective-permute-start.4
  237.2 42.0 %collective-permute-done.4 = f32[2,64,1,1,4096]{4,1,0,3,2:T(8,128)S(1)} collective-permute-done((f32[2,64,1,1,4096]{4,1,0,3,2:T(8,128)S(1)}, f32[2,64,1,1,4096]{4,1,0,3,2:T(8,128)S(1)}, u32[]{:S(2)}, u32[]{:S(2)}) %collective-permute-start.4) | collective-permute-done | bytes 2097184 | tf_op jit(solution)/shard_map/ppermute | solution.py:10
  279.2 0.2 fusion.53
  279.4 12.2 %collective-permute-start.5 = (f32[2,64,1,1,4096]{4,1,0,3,2:T(8,128)S(1)}, f32[2,64,1,1,4096]{4,1,0,3,2:T(8,128)}, u32[]{:S(2)}, u32[]{:S(2)}) collective-permute-start(f32[2,64,1,1,4096]{4,1,0,3,2:T(8,128)S(1)} %fusion.53), channel_id=1, source_target_pairs={{0,4},{1,5},{2,6},{3,7},{4,0},{5,1},{6,2},{7,3},{8,12},{9,13},{10,... | collective-permute-start | bytes 6291464 | tf_op jit(solution)/shard_map/ppermute | solution.py:10
  291.7 60.9 %collective-permute-done.5 = f32[2,64,1,1,4096]{4,1,0,3,2:T(8,128)} collective-permute-done((f32[2,64,1,1,4096]{4,1,0,3,2:T(8,128)S(1)}, f32[2,64,1,1,4096]{4,1,0,3,2:T(8,128)}, u32[]{:S(2)}, u32[]{:S(2)}) %collective-permute-start.5) | collective-permute-done | bytes 2097184 | tf_op jit(solution)/shard_map/ppermute | solution.py:10
  352.6 3.7 convolution_bitcast_fusion.1
  356.3 9.3 %multiply_add_fusion.1 = (f32[1,64,1,1,4096]{4,1,0,3,2:T(8,128)S(1)}, f32[1,64,1,1,4096]{4,1,0,3,2:T(8,128)S(1)}, f32[1,64,1,1,4096]{4,1,0,3,2:T(8,128)S(1)}) fusion(f32[4,2,64,4096]{3,2,1,0:T(8,128)} %param.8, f32[64]{0:T(128)S(1)} %get-tuple-element.41, f32[2,64,1,1,4096]{4,1,0,3,2:T(8,128)S(1)} %convolution_bitcast_fusion.1, f32[64]{0:T(128)S(1)} %get-tuple-element.40), kind=kLoop, calls=%fused_computation.28 | loop fusion | flops 2883584 | bytes 7340544 | tf_op jit(solution)/shard_map/add | solution.py:17
  365.6 5.0 multiply_subtract_fusion.1
  370.6 0.2 pad_maximum_fusion.3
  370.8 3.1 collective-permute-start.6
  373.9 37.7 %collective-permute-done.6 = f32[2,64,1,1,4096]{4,1,0,3,2:T(8,128)S(1)} collective-permute-done((f32[2,64,1,1,4096]{4,1,0,3,2:T(8,128)S(1)}, f32[2,64,1,1,4096]{4,1,0,3,2:T(8,128)S(1)}, u32[]{:S(2)}, u32[]{:S(2)}) %collective-permute-start.6) | collective-permute-done | bytes 2097184 | tf_op jit(solution)/shard_map/ppermute | solution.py:10
  411.6 0.2 fusion.52
  411.8 30.5 %collective-permute-start.7 = (f32[2,64,1,1,4096]{4,1,0,3,2:T(8,128)S(1)}, f32[2,64,1,1,4096]{4,1,0,3,2:T(8,128)}, u32[]{:S(2)}, u32[]{:S(2)}) collective-permute-start(f32[2,64,1,1,4096]{4,1,0,3,2:T(8,128)S(1)} %fusion.52), channel_id=1, source_target_pairs={{0,2},{1,3},{2,0},{3,1},{4,6},{5,7},{6,4},{7,5},{8,10},{9,11},{10,... | collective-permute-start | bytes 6291464 | tf_op jit(solution)/shard_map/ppermute | solution.py:10
  442.3 87.7 %collective-permute-done.7 = f32[2,64,1,1,4096]{4,1,0,3,2:T(8,128)} collective-permute-done((f32[2,64,1,1,4096]{4,1,0,3,2:T(8,128)S(1)}, f32[2,64,1,1,4096]{4,1,0,3,2:T(8,128)}, u32[]{:S(2)}, u32[]{:S(2)}) %collective-permute-start.7) | collective-permute-done | bytes 2097184 | tf_op jit(solution)/shard_map/ppermute | solution.py:10
  530.0 3.7 convolution_bitcast_fusion
  533.7 6.5 %multiply_subtract_fusion = (f32[1,64,1,1,4096]{4,1,0,3,2:T(8,128)S(1)}, f32[1,64,1,1,4096]{4,1,0,3,2:T(8,128)S(1)}) fusion(f32[2,64,1,1,4096]{4,1,0,3,2:T(8,128)S(1)} %convolution_bitcast_fusion, f32[4,2,64,4096]{3,2,1,0:T(8,128)} %param.8, f32[64]{0:T(128)S(1)} %fusion.51), kind=kLoop, calls=%fused_computation.26 | loop fusion | flops 1835008 | bytes 5243136 | tf_op jit(solution)/shard_map/sub | solution.py:25
  540.3 0.1 pad_maximum_fusion.4
  540.4 3.5 copy.8
  (5 shorter events, 0.0 us)
Async XLA Ops:
  0.0 107.8 %copy-start = (f32[4,64,64]{2,1,0:T(8,128)S(1)}, f32[4,64,64]{2,1,0:T(8,128)}, u32[]{:S(2)}) copy-start(f32[4,64,64]{2,1,0:T(8,128)} %param.9) | copy-start | bytes 196612
  10.4 49.0 %collective-permute-start = (f32[2,64,1,1,4096]{4,1,3,2,0:T(8,128)S(1)}, f32[2,64,1,1,4096]{4,1,3,2,0:T(8,128)S(1)}, u32[]{:S(2)}, u32[]{:S(2)}) collective-permute-start(f32[2,64,1,1,4096]{4,1,3,2,0:T(8,128)S(1)} %pad_maximum_fusion), channel_id=1, source_target_pairs={{0,128},{32,160},{64,192},{96,224},{128,0},{160,32},{192,64},{224,... | collective-permute-start | bytes 6291464 | tf_op jit(solution)/shard_map/ppermute | solution.py:10
  59.6 48.2 %collective-permute-start.1 = (f32[2,64,1,1,4096]{4,1,3,2,0:T(8,128)S(1)}, f32[2,64,1,1,4096]{4,1,3,2,0:T(8,128)}, u32[]{:S(2)}, u32[]{:S(2)}) collective-permute-start(f32[2,64,1,1,4096]{4,1,3,2,0:T(8,128)S(1)} %fusion.55), channel_id=1, source_target_pairs={{0,16},{1,17},{2,18},{3,19},{4,20},{5,21},{6,22},{7,23},{8,24},{9,... | collective-permute-start | bytes 6291464 | tf_op jit(solution)/shard_map/ppermute | solution.py:10
  126.0 45.7 %collective-permute-start.2 = (f32[2,64,1,1,4096]{4,1,0,3,2:T(8,128)S(1)}, f32[2,64,1,1,4096]{4,1,0,3,2:T(8,128)S(1)}, u32[]{:S(2)}, u32[]{:S(2)}) collective-permute-start(f32[2,64,1,1,4096]{4,1,0,3,2:T(8,128)S(1)} %pad_maximum_fusion.1), channel_id=1, source_target_pairs={{0,64},{32,96},{64,0},{96,32},{128,192},{160,224},{192,128},{224,1... | collective-permute-start | bytes 6291464 | tf_op jit(solution)/shard_map/ppermute | solution.py:10
  171.9 45.0 %collective-permute-start.3 = (f32[2,64,1,1,4096]{4,1,0,3,2:T(8,128)S(1)}, f32[2,64,1,1,4096]{4,1,0,3,2:T(8,128)}, u32[]{:S(2)}, u32[]{:S(2)}) collective-permute-start(f32[2,64,1,1,4096]{4,1,0,3,2:T(8,128)S(1)} %fusion.54), channel_id=1, source_target_pairs={{0,8},{1,9},{2,10},{3,11},{4,12},{5,13},{6,14},{7,15},{8,0},{9,1},... | collective-permute-start | bytes 6291464 | tf_op jit(solution)/shard_map/ppermute | solution.py:10
  235.2 44.0 %collective-permute-start.4 = (f32[2,64,1,1,4096]{4,1,0,3,2:T(8,128)S(1)}, f32[2,64,1,1,4096]{4,1,0,3,2:T(8,128)S(1)}, u32[]{:S(2)}, u32[]{:S(2)}) collective-permute-start(f32[2,64,1,1,4096]{4,1,0,3,2:T(8,128)S(1)} %pad_maximum_fusion.2), channel_id=1, source_target_pairs={{0,32},{32,0},{64,96},{96,64},{128,160},{160,128},{192,224},{224,1... | collective-permute-start | bytes 6291464 | tf_op jit(solution)/shard_map/ppermute | solution.py:10
  279.4 73.2 %collective-permute-start.5 = (f32[2,64,1,1,4096]{4,1,0,3,2:T(8,128)S(1)}, f32[2,64,1,1,4096]{4,1,0,3,2:T(8,128)}, u32[]{:S(2)}, u32[]{:S(2)}) collective-permute-start(f32[2,64,1,1,4096]{4,1,0,3,2:T(8,128)S(1)} %fusion.53), channel_id=1, source_target_pairs={{0,4},{1,5},{2,6},{3,7},{4,0},{5,1},{6,2},{7,3},{8,12},{9,13},{10,... | collective-permute-start | bytes 6291464 | tf_op jit(solution)/shard_map/ppermute | solution.py:10
  370.8 40.8 %collective-permute-start.6 = (f32[2,64,1,1,4096]{4,1,0,3,2:T(8,128)S(1)}, f32[2,64,1,1,4096]{4,1,0,3,2:T(8,128)S(1)}, u32[]{:S(2)}, u32[]{:S(2)}) collective-permute-start(f32[2,64,1,1,4096]{4,1,0,3,2:T(8,128)S(1)} %pad_maximum_fusion.3), channel_id=1, source_target_pairs={{0,128},{32,160},{64,192},{96,224},{128,0},{160,32},{192,64},{224,... | collective-permute-start | bytes 6291464 | tf_op jit(solution)/shard_map/ppermute | solution.py:10
  411.8 118.2 %collective-permute-start.7 = (f32[2,64,1,1,4096]{4,1,0,3,2:T(8,128)S(1)}, f32[2,64,1,1,4096]{4,1,0,3,2:T(8,128)}, u32[]{:S(2)}, u32[]{:S(2)}) collective-permute-start(f32[2,64,1,1,4096]{4,1,0,3,2:T(8,128)S(1)} %fusion.52), channel_id=1, source_target_pairs={{0,2},{1,3},{2,0},{3,1},{4,6},{5,7},{6,4},{7,5},{8,10},{9,11},{10,... | collective-permute-start | bytes 6291464 | tf_op jit(solution)/shard_map/ppermute | solution.py:10
where the time goes:
time: 545 us; the launch traced here: 544 us
  waiting for transfers between devices  408 us (75%)
  other arithmetic  58.1 us (11%)
  starting transfers between devices  55.8 us (10%)
  matrix products  14.8 us (3%)
  local copies, waits for them, and re-layouts  6.91 us (1%)
    ppermute x8, waiting for transfers between devices, partner(): lax.ppermute(x, axis, [(i, i ^ 1 << distance) for i in range(lax.axis_siz...  408 us
    ppermute x8, starting transfers between devices, partner(): lax.ppermute(x, axis, [(i, i ^ 1 << distance) for i in range(lax.axis_siz...  55.8 us
    add x4, other arithmetic, rotate_in(): values[0] * cosine + values[1] * sine_part  34.6 us
    sub x3, other arithmetic, rotate_in(): values[1] * cosine - values[0] * sine_part  15.1 us
    dot_general x4, matrix products, per_device(): jnp.einsum('tk,rkabq->rtabq', blocks, summed, precision=lax.Precision.HIG...  14.8 us
  transfers between devices with their start and end apart: 8, of which 8 were waited for; matrix products, arithmetic and copies ran while one was open for 0% of the time, Pallas kernels for 0%

commit v1 on v0

v1 whole, which is shorter than its diff:
```python
import jax
import jax.numpy as jnp
from jax import lax
from jax.experimental import pallas as pl
from jax.experimental.pallas import tpu as pltpu
from jax.sharding import PartitionSpec as P

MESH = pl.DeviceIdType.MESH
F32 = jnp.float32
BF16 = jnp.bfloat16
K = 64
LANES = 128


def flip(bit, other):
    return bit + other - 2 * bit * other


def flip_bits(value, mask, bits):
    total = 0
    for n in range(bits):
        total = total + (1 << n) * flip(value // (1 << n) % 2, mask // (1 << n) % 2)
    return total


def lane_bit(shape, width):
    return lax.broadcasted_iota(jnp.int32, shape, len(shape) - 1) // width % 2 == 0


def lane_transpose(parts):
    low64 = lane_bit(parts[0].shape, 64)
    low32 = lane_bit(parts[0].shape, 32)
    a, b, c, d = parts
    a, c = jnp.where(low64, a, pltpu.roll(c, 64, 1)), jnp.where(low64, pltpu.roll(a, 64, 1), c)
    b, d = jnp.where(low64, b, pltpu.roll(d, 64, 1)), jnp.where(low64, pltpu.roll(b, 64, 1), d)
    a, b = jnp.where(low32, a, pltpu.roll(b, 32, 1)), jnp.where(low32, pltpu.roll(a, 96, 1), b)
    c, d = jnp.where(low32, c, pltpu.roll(d, 32, 1)), jnp.where(low32, pltpu.roll(c, 96, 1), d)
    return a, b, c, d


def pack(re, im):
    return lane_transpose((re[:32], re[32:], im[:32], im[32:]))


def unpack(parts):
    a, b, c, d = lane_transpose(parts)
    return jnp.concatenate([a, b], 0), jnp.concatenate([c, d], 0)


def turn(re, im, cos, sin):
    return re * cos - im * sin, re * sin + im * cos


def split_rows(re, im):
    both = jnp.concatenate([re, im], 1)
    high = both.astype(BF16)
    low = (both - high.astype(F32)).astype(BF16)
    return jnp.concatenate([high, low, high], 0)


def split_columns(blocks):
    high = blocks.astype(BF16).astype(F32)
    low = blocks - high
    return jnp.concatenate([high, high, low], 1).astype(BF16)


def kernel(
    coeff, phase_x, phase_y, phase_q, interp, out,
    field, first, second, send_a, recv_a, send_b, recv_b, recv_z, recv_x,
    state, factor, x_cos, x_sin, y_cos, y_sin, q_own, q_cos, q_sin, last, q_last, staged,
    maps, own_map,
    field_sem, q_sem, first_send, first_recv, second_send, second_recv,
    a_send, a_recv, b_send, b_recv, z_send, z_recv, x_send, x_recv, out_sem,
):
    gx, gy = lax.axis_index("gx"), lax.axis_index("gy")
    x2, x1, x0 = gx // 4, gx // 2 % 2, gx % 2
    y4, y3, y2, y1, core = gy // 16, gy // 8 % 2, gy // 4 % 2, gy // 2 % 2, gy % 2
    z = 4 * y2 + 2 * y1 + x0
    group = 2 * x1 + y3

    def device(fx2=0, fx1=0, fx0=0, fy4=0, fy3=0, fy2=0, fy1=0):
        return (
            4 * flip(x2, fx2) + 2 * flip(x1, fx1) + flip(x0, fx0),
            16 * flip(y4, fy4) + 8 * flip(y3, fy3) + 4 * flip(y2, fy2) + 2 * flip(y1, fy1) + core,
        )

    def spread_device(slot):
        return device(
            fy2=slot // 16, fy1=slot // 8 % 2, fx0=slot // 4 % 2, fx1=slot // 2 % 2, fy3=slot % 2
        )

    def gather_device(slot):
        return device(
            fy4=slot // 16, fx0=slot // 8 % 2, fy2=slot // 4 % 2, fx1=slot // 2 % 2, fy3=slot % 2
        )

    barrier = pltpu.get_barrier_semaphore()

    def load(i):
        for fx in range(2):
            for fy in range(2):
                block = 16 * flip(x2, fx) + 8 * flip(y4, fy) + flip_bits(z, i, 3)
                yield pltpu.make_async_copy(
                    coeff.at[:, :, block, :], field.at[i, fx, fy], field_sem.at[i, fx, fy]
                )

    for i in range(8):
        for copy in load(i):
            copy.start()
    own_block = 16 * x2 + 8 * y4 + z
    own_copy = pltpu.make_async_copy(
        phase_q.at[:, :, :, pl.ds(pl.multiple_of(own_block * LANES, LANES), LANES)], q_own, q_sem.at[0]
    )
    own_copy.start()
    last_copy = pltpu.make_async_copy(phase_q.at[3, 1], q_last, q_sem.at[1])
    last_copy.start()

    @pl.loop(1, 32)
    def _(slot):
        pl.semaphore_signal(barrier, inc=1, device_id=spread_device(slot), device_id_type=MESH)

    @pl.loop(16, 32)
    def _(slot):
        pl.semaphore_signal(barrier, inc=1, device_id=gather_device(slot), device_id_type=MESH)

    pl.semaphore_signal(barrier, inc=1, device_id=device(fx2=1), device_id_type=MESH)

    def columns(row):
        wide = jnp.broadcast_to(jnp.concatenate([row, row], 1), (LANES, LANES))
        return wide.T[:K]

    angle = phase_x[0, 0, pl.ds(gx, 1), :] + phase_y[0, 0, pl.ds(gy, 1), :]
    in_cos, in_sin = columns(jnp.cos(angle)), columns(-jnp.sin(angle))
    out_angle = columns(phase_x[3, 1, pl.ds(gx, 1), :] + phase_y[3, 1, pl.ds(gy, 1), :])

    def rotate(i, fx, fy):
        re, im = turn(field[i, fx, fy, 0], field[i, fx, fy, 1], in_cos, in_sin)
        field[i, fx, fy, 0] = re
        field[i, fx, fy, 1] = im

    pl.semaphore_wait(barrier, 48)

    x_first = [i % 2 == 0 for i in range(8)]
    partner_x, partner_y, partner_z = device(fx2=1), device(fy4=1), device(fy1=1)

    def first_copy(i):
        return pltpu.make_async_remote_copy(
            field.at[i, 1] if x_first[i] else field.at[i, :, 1],
            first.at[i], first_send.at[i], first_recv.at[i],
            device_id=partner_x if x_first[i] else partner_y, device_id_type=MESH,
        )

    def second_copy(i):
        return pltpu.make_async_remote_copy(
            field.at[i, 0, 1] if x_first[i] else field.at[i, 1, 0],
            second.at[i], second_send.at[i], second_recv.at[i],
            device_id=partner_y if x_first[i] else partner_x, device_id_type=MESH,
        )

    order = [7, 6, 5, 4, 3, 2, 1, 0]
    for i in order:
        copies = list(load(i))
        for copy in copies:
            copy.wait()
        for fx, fy in ((1, 1), (1, 0) if x_first[i] else (0, 1)):
            rotate(i, fx, fy)
        first_copy(i).start()
    for i in order:
        for fx, fy in ((0, 0), (0, 1) if x_first[i] else (1, 0)):
            rotate(i, fx, fy)

    for l in range(3):
        difference = phase_x[l, 1] - phase_x[l + 1, 0]
        x_cos[l] = jnp.cos(difference)
        x_sin[l] = jnp.sin(difference)
        difference = phase_y[l, 1] - phase_y[l + 1, 0]
        y_cos[l] = jnp.cos(difference)
        y_sin[l] = jnp.sin(difference)

    @pl.loop(0, 32)
    def _(n):
        for l in range(3):
            rows = []
            for high in range(2):
                if l < 2:
                    a = n // 8 * 2 + high
                else:
                    a = n // 16 * 4 + high * 2 + n // 8 % 2
                for low in range(2):
                    b = n % 8 * 4 + low * 2 + core
                    xc, xs = x_cos[l, pl.ds(a, 1), :], x_sin[l, pl.ds(a, 1), :]
                    yc, ys = y_cos[l, pl.ds(b, 1), :], y_sin[l, pl.ds(b, 1), :]
                    row = jnp.concatenate(turn(xc, xs, yc, ys), 1)
                    rows.append(jnp.broadcast_to(row, (32, LANES)))
            factor[l, n] = jnp.concatenate(rows, 0).T

    own_copy.wait()
    for l in range(4):
        value = -q_own[0, 0] if l == 0 else q_own[l - 1, 1] - q_own[l, 0]
        value = pltpu.roll(value, (128 - 32 * group) % 128, 1)
        value = jnp.where(lax.broadcasted_iota(jnp.int32, value.shape, 1) < 32, value, 0.0)
        value = value + pltpu.roll(value, 32, 1)
        value = value + pltpu.roll(value, 64, 1)
        q_cos[l] = jnp.cos(value)
        q_sin[l] = jnp.sin(value)
    maps[...] = jnp.concatenate([split_columns(interp[c]) for c in range(4)], 0)
    own_map[...] = split_columns(interp[2 * x2 + y1])

    for i in order:
        first_copy(i).wait()
        fx, fy = (0, 1) if x_first[i] else (1, 0)
        field[i, fx, fy] = field[i, fx, fy] + first[i, 1]
        second_copy(i).start()
        field[i, 0, 0] = field[i, 0, 0] + first[i, 0]

    def spread_copy(slot):
        return pltpu.make_async_remote_copy(
            send_a.at[slot], recv_a.at[slot], a_send, a_recv,
            device_id=spread_device(slot), device_id_type=MESH,
        )

    for i in order:
        second_copy(i).wait()
        parts = pack(field[i, 0, 0, 0] + second[i, 0], field[i, 0, 0, 1] + second[i, 1])
        for g in range(4):
            send_a[4 * i + flip_bits(group, g, 2)] = parts[g]
        for g in range(4):
            if i == 0 and g == 0:
                recv_a[0] = send_a[0]
            else:
                spread_copy(4 * i + g).start()

    last_copy.wait()

    @pl.loop(0, 32)
    def _(block):
        value = out_angle + q_last[:, pl.ds(pl.multiple_of(block * LANES, LANES), LANES)]
        last[block, 0] = jnp.cos(value)
        last[block, 1] = jnp.sin(value)

    pltpu.make_async_remote_copy(
        send_a.at[pl.ds(1, 31)], recv_a.at[pl.ds(1, 31)], a_send, a_recv,
        device_id=partner_x, device_id_type=MESH,
    ).wait()

    def mapped(re, im):
        return jnp.dot(maps[...], split_rows(re, im), preferred_element_type=F32)

    def add_turned(total, values, l, place):
        for c in range(4):
            cos, sin = factor[l, place(c), :K], factor[l, place(c), K:]
            re, im = turn(values[c * K:(c + 1) * K, :LANES], values[c * K:(c + 1) * K, LANES:], cos, sin)
            total[c] = (re, im) if total[c] is None else (total[c][0] + re, total[c][1] + im)

    def finish(re, im, l):
        return turn(re, im, q_cos[l], q_sin[l])

    @pl.loop(0, 2)
    def _(c2):
        total = [None] * 4
        for s1 in range(2):
            for s3 in range(2):
                messages = []
                for s0 in range(2):
                    for t1 in range(2):
                        place = 4 * flip(y2, c2) + 2 * flip(y1, t1) + flip(x0, s0)
                        messages.append(recv_a[4 * place + 2 * flip(x1, s1) + flip(y3, s3)])
                re, im = finish(*unpack(messages), 0)
                add_turned(
                    total, mapped(re, im), 0,
                    lambda c: (c // 2 * 2 + s1) * 8 + c % 2 * 4 + s3 * 2 + c2,
                )
        for c in range(4):
            re, im = finish(*total[c], 1)
            state[0, 2 * c + c2, 0] = re
            state[0, 2 * c + c2, 1] = im

    @pl.loop(0, 4)
    def _(c):
        total = [None] * 4
        for s2 in range(2):
            add_turned(
                total, mapped(state[0, 2 * c + s2, 0], state[0, 2 * c + s2, 1]), 1,
                lambda d: (c // 2 * 2 + d // 2) * 8 + c % 2 * 4 + d % 2 * 2 + s2,
            )
        low = lane_bit((K, LANES), 64)
        for d3 in range(2):
            re, im = finish(*(
                jnp.where(low, a + pltpu.roll(a, 64, 1), b + pltpu.roll(b, 64, 1))
                for a, b in zip(total[d3], total[2 + d3])
            ), 2)
            state[1, 2 * c + d3, 0] = re
            state[1, 2 * c + d3, 1] = im

    def gather_copy(slot):
        return pltpu.make_async_remote_copy(
            send_b.at[slot], recv_b.at[slot // 4, slot % 4], b_send, b_recv.at[slot // 4],
            device_id=gather_device(slot), device_id_type=MESH,
        )

    for r4 in range(2):
        for r3 in range(2):
            d4, d3 = flip(y4, r4), flip(y3, r3)
            total = [None] * 4
            for s in range(2):
                n = 4 * s + 2 * d4 + d3
                add_turned(
                    total, mapped(state[1, n, 0], state[1, n, 1]), 2,
                    lambda c: (s * 2 + c // 2) * 8 + 4 * d4 + 2 * d3 + c % 2,
                )
            low = lane_bit((K, LANES), 32)
            for c2 in range(2):
                re, im = finish(*(
                    jnp.where(low, a + pltpu.roll(a, 96, 1), b + pltpu.roll(b, 32, 1))
                    for a, b in zip(total[c2], total[2 + c2])
                ), 3)
                parts = pack(re, im)
                for e1 in range(2):
                    for e0 in range(2):
                        slot = 16 * r4 + 8 * flip(x0, e0) + 4 * flip(y2, c2) + 2 * flip(x1, e1) + r3
                        send_b[slot] = parts[2 * e1 + e0]
            for slot in range(32):
                if slot // 16 == r4 and slot % 2 == r3:
                    if slot == 0:
                        recv_b[0, 0] = send_b[0]
                    else:
                        gather_copy(slot).start()

    def z_copy(i):
        return pltpu.make_async_remote_copy(
            recv_b.at[i], recv_z.at[i], z_send.at[i], z_recv.at[i],
            device_id=partner_z, device_id_type=MESH,
        )

    def x_copy(i):
        return pltpu.make_async_remote_copy(
            recv_b.at[i] if i < 8 else recv_z.at[i - 8], recv_x.at[i], x_send.at[i], x_recv.at[i],
            device_id=partner_x, device_id_type=MESH,
        )

    def result_copy(block):
        return pltpu.make_async_copy(staged.at[block], out.at[:, :, block, :], out_sem.at[block])

    def expand(source, i, fx, fz):
        block = (
            16 * flip(x2, fx) + 8 * flip(y4, i // 4) + 4 * flip(y2, i % 2) + 2 * flip(y1, fz)
            + flip(x0, i // 2 % 2)
        )
        re, im = unpack([source[flip_bits(group, g, 2)] for g in range(4)])
        values = jnp.dot(own_map[...], split_rows(re, im), preferred_element_type=F32)
        re, im = turn(values[:, :LANES], values[:, LANES:], last[block, 0], last[block, 1])
        staged[block, 0] = re
        staged[block, 1] = im
        result_copy(block).start()

    for i in range(8):
        arrived = recv_b.at[0, pl.ds(1, 3)] if i == 0 else recv_b.at[i]
        pltpu.make_async_remote_copy(
            arrived, arrived, b_send, b_recv.at[i], device_id=partner_x, device_id_type=MESH
        ).wait_recv()
        z_copy(i).start()
        x_copy(i).start()
    for i in range(8):
        expand(recv_b.at[i], i, 0, 0)
    for i in range(8):
        z_copy(i).wait_recv()
        x_copy(8 + i).start()
        expand(recv_z.at[i], i, 0, 1)
    for i in range(16):
        x_copy(i).wait_recv()
        expand(recv_x.at[i], i % 8, 1, i // 8)
    for i in range(8):
        z_copy(i).wait_send()
    for i in range(16):
        x_copy(i).wait_send()
    pltpu.make_async_remote_copy(
        send_b.at[pl.ds(1, 31)], send_b.at[pl.ds(1, 31)], b_send, b_recv.at[0],
        device_id=partner_x, device_id_type=MESH,
    ).wait_send()
    for block in range(32):
        result_copy(block).wait()


def per_device(coeff, phase_x, phase_y, phase_q, interp):
    field = (2, K, LANES)
    message = (32, LANES)
    dma = pltpu.SemaphoreType.DMA
    result = pl.pallas_call(
        kernel,
        out_shape=jax.ShapeDtypeStruct((2, K, 32, LANES), F32),
        in_specs=[
            pl.BlockSpec(memory_space=pl.ANY),
            pl.BlockSpec(memory_space=pltpu.VMEM),
            pl.BlockSpec(memory_space=pltpu.VMEM),
            pl.BlockSpec(memory_space=pl.ANY),
            pl.BlockSpec(memory_space=pltpu.VMEM),
        ],
        out_specs=pl.BlockSpec(memory_space=pl.ANY),
        scratch_shapes=[
            pltpu.VMEM((8, 2, 2, *field), F32),
            pltpu.VMEM((8, 2, *field), F32),
            pltpu.VMEM((8, *field), F32),
            pltpu.VMEM((32, *message), F32),
            pltpu.VMEM((32, *message), F32),
            pltpu.VMEM((32, *message), F32),
            pltpu.VMEM((8, 4, *message), F32),
            pltpu.VMEM((8, 4, *message), F32),
            pltpu.VMEM((16, 4, *message), F32),
            pltpu.VMEM((2, 8, *field), F32),
            pltpu.VMEM((3, 32, LANES, LANES), F32),
            pltpu.VMEM((3, 8, K), F32),
            pltpu.VMEM((3, 8, K), F32),
            pltpu.VMEM((3, 32, K), F32),
            pltpu.VMEM((3, 32, K), F32),
            pltpu.VMEM((4, 2, K, LANES), F32),
            pltpu.VMEM((4, K, LANES), F32),
            pltpu.VMEM((4, K, LANES), F32),
            pltpu.VMEM((32, *field), F32),
            pltpu.VMEM((K, 32 * LANES), F32),
            pltpu.VMEM((32, *field), F32),
            pltpu.VMEM((4 * K, 3 * K), BF16),
            pltpu.VMEM((K, 3 * K), BF16),
            dma((8, 2, 2)), dma((2,)), dma((8,)), dma((8,)), dma((8,)), dma((8,)),
            dma, dma, dma, dma((8,)), dma((8,)), dma((8,)), dma((16,)), dma((16,)), dma((32,)),
        ],
        compiler_params=pltpu.CompilerParams(
            collective_id=0, has_side_effects=True, vmem_limit_bytes=48 * 1024 * 1024
        ),
    )(
        coeff.reshape(2, K, 32, LANES),
        phase_x.transpose(0, 1, 3, 2),
        phase_y.transpose(0, 1, 3, 2),
        phase_q,
        interp,
    )
    return result.reshape(2, K, 1, 1, 32 * LANES)


def solution(mesh):
    placed = (P(None, None, "gx", "gy", None), P(), P(), P(), P())
    return jax.shard_map(
        per_device,
        mesh=mesh,
        in_specs=placed,
        out_specs=P(None, None, "gx", "gy", None),
        check_vma=False,
    )
```

time: 545 us -> 93.4 us (0.17)
  waiting for transfers between devices: 408 us -> 0 us
  Pallas kernels: 0 us -> 86.6 us
  other arithmetic: 58.1 us -> 0 us
  starting transfers between devices: 55.8 us -> 0 us
  matrix products: 14.8 us -> 0 us
    ppermute x8 -> x0, waiting for transfers between devices: 408 us -> none  [partner(): lax.ppermute(x, axis, [(i, i ^ 1 << distance) for i in range(lax.axis_siz...]
    pallas_call x0 -> x1, Pallas kernels: none -> 86.6 us  [per_device(): pl.pallas_call(kernel, out_shape=jax.ShapeDtypeStruct((2, K, 32, LANES),...]
    ppermute x8 -> x0, starting transfers between devices: 55.8 us -> none  [partner(): lax.ppermute(x, axis, [(i, i ^ 1 << distance) for i in range(lax.axis_siz...]
    add x13 -> x0, other arithmetic: 35.6 us -> none  [the longest x4 34.6 us: rotate_in(): values[0] * cosine + values[1] * sine_part]
    sub x4 -> x0, other arithmetic: 21.6 us -> none  [the longest x3 15.1 us: rotate_in(): values[1] * cosine - values[0] * sine_part]
    dot_general x4 -> x0, matrix products: 14.8 us -> none  [per_device(): jnp.einsum('tk,rkabq->rtabq', blocks, summed, precision=lax.Precision.HIG...]
    unnamed x2 -> x9, local copies, waits for them, and re-layouts: 0.01 us -> 5.48 us
  transfers between devices with their start and end apart: 8 -> 0, of which waited for: 8 -> 0; matrix products, arithmetic and copies ran while one was open for 0% -> 0% of each run, Pallas kernels for 0% -> 0%
where the time goes in v1:
time: 93.4 us; the launch traced here: 92.1 us
  Pallas kernels  86.6 us (93%)
  local copies, waits for them, and re-layouts  5.48 us (6%)
    pallas_call x1, Pallas kernels, per_device(): pl.pallas_call(kernel, out_shape=jax.ShapeDtypeStruct((2, K, 32, LANES),...  86.6 us
    unnamed x9, local copies, waits for them, and re-layouts  5.48 us

profile of v1, /device:TPU:8, one launch (start us, length us, event | category | flops | bytes accessed | tf_op | source)
XLA Modules:
  0.0 92.1 jit_solution(6398518660968283032)
XLA Ops:
  0.0 0.0 copy-start
  0.0 1.6 %copy-done = f32[2,64,1,1,4096]{4,3,2,1,0:T(1,128)S(1)} copy-done((f32[2,64,1,1,4096]{4,3,2,1,0:T(1,128)S(1)}, f32[2,64,1,1,4096]{4,3,2,1,0:T(1,128)}, u32[]{:S(2)}) %copy-start) | copy-done | bytes 2097176
  1.6 0.0 copy-start.1
  1.6 0.9 copy-done.1
  2.5 0.0 copy-start.2
  2.5 0.9 copy-done.2
  3.4 0.0 copy-start.3
  3.4 0.8 copy-done.3
  4.2 86.6 %shard_map.55 = f32[2,64,32,128]{3,2,1,0:T(8,128)S(1)} custom-call(f32[2,64,32,128]{3,2,1,0:T(8,128)S(1)} %bitcast.5, f32[4,2,8,64]{3,2,1,0:T(8,128)S(1)} %bitcast.7, f32[4,2,32,64]{3,2,1,0:T(8,128)S(1)} %bitcast.6, f32[4,2,64,4096]{3,2,1,0:T(8,128)} %phase_q.1, f32[4,64,64]{2,1,0:T(8,128)S(1)} %copy-done.2), custom_call_target="tpu_custom_call" | custom-call | tf_op jit(solution)/shard_map/pallas_call | solution.py:388
  90.7 1.3 %copy.8 = f32[2,64,1,1,4096]{4,3,2,1,0:T(1,128)} copy(f32[2,64,1,1,4096]{4,3,2,1,0:T(1,128)S(1)} %bitcast.4) | data formatting | bytes 4194304
Async XLA Ops:
  0.0 1.6 %copy-start = (f32[2,64,1,1,4096]{4,3,2,1,0:T(1,128)S(1)}, f32[2,64,1,1,4096]{4,3,2,1,0:T(1,128)}, u32[]{:S(2)}) copy-start(f32[2,64,1,1,4096]{4,3,2,1,0:T(1,128)} %param.5) | copy-start | bytes 6291460
  1.6 0.9 copy-start.1
  2.5 0.9 copy-start.2
  3.4 0.8 copy-start.3

commit v2 on v1

v2 whole, which is shorter than its diff:
```python
import jax
import jax.numpy as jnp
import numpy as np
from jax import lax
from jax.experimental import pallas as pl
from jax.experimental.pallas import tpu as pltpu
from jax.sharding import PartitionSpec as P

MESH = pl.DeviceIdType.MESH
F32 = jnp.float32
BF16 = jnp.bfloat16
K = 64
LANES = 128
ORDER = (4, 5, 6, 2, 3, 7, 1, 0)
AHEAD = 4
LAG = 3
BEHIND = 3
GATHER_ORDER = (0, 4, 2, 6, 3, 7, 1, 5)


def flip(bit, other):
    return bit + other - 2 * bit * other


def flip_bits(value, mask, bits):
    total = 0
    for n in range(bits):
        total = total + (1 << n) * flip(value // (1 << n) % 2, mask // (1 << n) % 2)
    return total


def lane_bit(shape, width):
    return lax.broadcasted_iota(jnp.int32, shape, len(shape) - 1) // width % 2 == 0


def lane_transpose(parts):
    low64 = lane_bit(parts[0].shape, 64)
    low32 = lane_bit(parts[0].shape, 32)
    a, b, c, d = parts
    a, c = jnp.where(low64, a, pltpu.roll(c, 64, 1)), jnp.where(low64, pltpu.roll(a, 64, 1), c)
    b, d = jnp.where(low64, b, pltpu.roll(d, 64, 1)), jnp.where(low64, pltpu.roll(b, 64, 1), d)
    a, b = jnp.where(low32, a, pltpu.roll(b, 32, 1)), jnp.where(low32, pltpu.roll(a, 96, 1), b)
    c, d = jnp.where(low32, c, pltpu.roll(d, 32, 1)), jnp.where(low32, pltpu.roll(c, 96, 1), d)
    return a, b, c, d


def pack(re, im):
    return lane_transpose((re[:32], re[32:], im[:32], im[32:]))


def unpack(parts):
    a, b, c, d = lane_transpose(parts)
    return jnp.concatenate([a, b], 0), jnp.concatenate([c, d], 0)


def cos_sin(angle):
    turns = jnp.round(angle * (2 / np.pi))
    rest = angle - turns * 1.5703125
    rest = rest - turns * 4.837512969970703125e-4
    rest = rest - turns * 7.54978995489188216e-8
    square = rest * rest
    sine = rest + rest * square * (
        -1.6666654611e-1 + square * (8.3321608736e-3 + square * -1.9515295891e-4)
    )
    cosine = 1.0 - 0.5 * square + square * square * (
        4.166664568298827e-2 + square * (-1.388731625493765e-3 + square * 2.443315711809948e-5)
    )
    quarter = turns.astype(jnp.int32) & 3
    odd = (quarter & 1) == 1
    cos, sin = jnp.where(odd, sine, cosine), jnp.where(odd, cosine, sine)
    cos = jnp.where((quarter == 1) | (quarter == 2), -cos, cos)
    return cos, jnp.where(quarter >= 2, -sin, sin)


def turn(re, im, cos, sin):
    return re * cos - im * sin, re * sin + im * cos


def split_rows(re, im):
    both = jnp.concatenate([re, im], 1)
    high = both.astype(BF16)
    low = (both - high.astype(F32)).astype(BF16)
    return jnp.concatenate([high, low, high], 0)


def split_columns(blocks):
    high = blocks.astype(BF16).astype(F32)
    low = blocks - high
    return jnp.concatenate([high, high, low], 1).astype(BF16)


def kernel(
    coeff, x_hbm, y_hbm, phase_q, interp_hbm, out,
    phase_x, phase_y, interp, field, first, second, send_a, recv_a, send_b, recv_b, recv_z, recv_x,
    state, factor_x, factor_y, factor, x_cos, x_sin, y_cos, y_sin, q_own, q_cos, q_sin, last, q_last, staged,
    maps, own_map,
    small_sem, field_sem, q_sem, first_send, first_recv, second_send, second_recv,
    a_send, a_recv, b_send, b_recv, z_send, z_recv, x_send, x_recv, out_sem,
):
    gx, gy = lax.axis_index("gx"), lax.axis_index("gy")
    x2, x1, x0 = gx // 4, gx // 2 % 2, gx % 2
    y4, y3, y2, y1, core = gy // 16, gy // 8 % 2, gy // 4 % 2, gy // 2 % 2, gy % 2
    z = 4 * y2 + 2 * y1 + x0
    group = 2 * x1 + y3

    def device(fx2=0, fx1=0, fx0=0, fy4=0, fy3=0, fy2=0, fy1=0):
        return (
            4 * flip(x2, fx2) + 2 * flip(x1, fx1) + flip(x0, fx0),
            16 * flip(y4, fy4) + 8 * flip(y3, fy3) + 4 * flip(y2, fy2) + 2 * flip(y1, fy1) + core,
        )

    def spread_device(slot):
        return device(
            fy2=slot // 16, fy1=slot // 8 % 2, fx0=slot // 4 % 2, fx1=slot // 2 % 2, fy3=slot % 2
        )

    def gather_device(slot):
        return device(
            fy4=slot // 16, fx0=slot // 8 % 2, fy2=slot // 4 % 2, fy1=slot // 4 % 2,
            fx1=slot // 2 % 2, fy3=slot % 2,
        )

    barrier = pltpu.get_barrier_semaphore()

    def load(i):
        for fx in range(2):
            for fy in range(2):
                block = 16 * flip(x2, fx) + 8 * flip(y4, fy) + flip_bits(z, i, 3)
                yield pltpu.make_async_copy(
                    coeff.at[:, :, block, :], field.at[i, fx, fy], field_sem.at[i]
                )

    small_copies = [
        pltpu.make_async_copy(source, target, small_sem.at[n])
        for n, (source, target) in enumerate(
            ((x_hbm, phase_x), (y_hbm, phase_y), (interp_hbm, interp))
        )
    ]
    for copy in small_copies:
        copy.start()
    for i in ORDER:
        for copy in load(i):
            copy.start()
    for slot in range(1, 32):
        pl.semaphore_signal(barrier, inc=1, device_id=spread_device(slot), device_id_type=MESH)
    for slot in range(16, 32):
        pl.semaphore_signal(barrier, inc=1, device_id=gather_device(slot), device_id_type=MESH)
    pl.semaphore_signal(barrier, inc=1, device_id=device(fx2=1), device_id_type=MESH)
    own_block = 16 * x2 + 8 * y4 + z
    own_copy = pltpu.make_async_copy(
        phase_q.at[:, :, :, pl.ds(pl.multiple_of(own_block * LANES, LANES), LANES)], q_own, q_sem.at[0]
    )
    own_copy.start()
    last_copy = pltpu.make_async_copy(phase_q.at[3, 1], q_last, q_sem.at[1])
    last_copy.start()

    def columns(row):
        wide = jnp.broadcast_to(jnp.concatenate([row, row], 1), (LANES, LANES))
        return wide.T[:K]

    for copy in small_copies:
        copy.wait()
    angle = phase_x[0, 0, pl.ds(gx, 1), :] + phase_y[0, 0, pl.ds(gy, 1), :]
    in_cos, in_sin = (columns(part) for part in cos_sin(-angle))
    out_angle = columns(phase_x[3, 1, pl.ds(gx, 1), :] + phase_y[3, 1, pl.ds(gy, 1), :])

    def rotate(i, fx, fy):
        re, im = turn(field[i, fx, fy, 0], field[i, fx, fy, 1], in_cos, in_sin)
        field[i, fx, fy, 0] = re
        field[i, fx, fy, 1] = im

    pl.semaphore_wait(barrier, 48)

    x_first = [ORDER.index(i) % 2 == 0 for i in range(8)]
    partner_x, partner_y, partner_z = device(fx2=1), device(fy4=1), device(fy1=1)

    def first_copy(i):
        return pltpu.make_async_remote_copy(
            field.at[i, 1] if x_first[i] else field.at[i, :, 1],
            first.at[i], first_send, first_recv.at[i],
            device_id=partner_x if x_first[i] else partner_y, device_id_type=MESH,
        )

    def second_copy(i):
        return pltpu.make_async_remote_copy(
            field.at[i, 0, 1] if x_first[i] else field.at[i, 1, 0],
            second.at[i], second_send, second_recv.at[i],
            device_id=partner_y if x_first[i] else partner_x, device_id_type=MESH,
        )

    def part_factors():
        for l in range(3):
            difference = phase_x[l, 1] - phase_x[l + 1, 0]
            x_cos[l], x_sin[l] = cos_sin(difference)
            difference = phase_y[l, 1] - phase_y[l + 1, 0]
            y_cos[l], y_sin[l] = cos_sin(difference)

    def edge_factors(l):
        def rows(cos, sin, places, count):
            return [
                jnp.broadcast_to(
                    jnp.concatenate([cos[l, pl.ds(p, 1), :], sin[l, pl.ds(p, 1), :]], 1), (count, LANES)
                )
                for p in places
            ]

        @pl.loop(0, 4, unroll=True)
        def _(n):
            places = [2 * n + h if l < 2 else n // 2 * 4 + h * 2 + n % 2 for h in range(2)]
            factor_x[l, n] = jnp.concatenate(rows(x_cos, x_sin, places, 64), 0).T

        @pl.loop(0, 8, unroll=True)
        def _(n):
            places = [4 * n + 2 * h + core for h in range(2)] * 2
            factor_y[l, n] = jnp.concatenate(rows(y_cos, y_sin, places, 32), 0).T

    def level_factors(l):
        @pl.loop(0, 32, unroll=4)
        def _(n):
            x, y = n // 8, n % 8
            cos, sin = turn(
                factor_x[l, x, :K], factor_x[l, x, K:], factor_y[l, y, :K], factor_y[l, y, K:]
            )
            factor[l, n, :K] = cos
            factor[l, n, K:] = sin

    def small_factors():
        own_copy.wait()
        for l in range(4):
            value = -q_own[0, 0] if l == 0 else q_own[l - 1, 1] - q_own[l, 0]
            value = pltpu.roll(value, (128 - 32 * group) % 128, 1)
            value = jnp.where(lax.broadcasted_iota(jnp.int32, value.shape, 1) < 32, value, 0.0)
            value = value + pltpu.roll(value, 32, 1)
            value = value + pltpu.roll(value, 64, 1)
            q_cos[l], q_sin[l] = cos_sin(value)
        maps[...] = jnp.concatenate([split_columns(interp[c]) for c in range(4)], 0)
        own_map[...] = split_columns(interp[2 * x2 + y1])

    def last_factors():
        @pl.loop(0, 32, unroll=4)
        def _(block):
            value = out_angle + q_last[:, pl.ds(pl.multiple_of(block * LANES, LANES), LANES)]
            last[block, 0], last[block, 1] = cos_sin(value)

    def start_first(i):
        pltpu.make_async_copy(field.at[i], field.at[i], field_sem.at[i]).wait()
        for fx, fy in ((1, 1), (1, 0) if x_first[i] else (0, 1)):
            rotate(i, fx, fy)
        first_copy(i).start()
        for fx, fy in ((0, 0), (0, 1) if x_first[i] else (1, 0)):
            rotate(i, fx, fy)

    def spread_copy(slot):
        return pltpu.make_async_remote_copy(
            send_a.at[slot], recv_a.at[slot], a_send, a_recv,
            device_id=spread_device(slot), device_id_type=MESH,
        )

    def start_second(i):
        first_copy(i).wait_recv()
        fx, fy = (0, 1) if x_first[i] else (1, 0)
        field[i, fx, fy] = field[i, fx, fy] + first[i, 1]
        second_copy(i).start()
        field[i, 0, 0] = field[i, 0, 0] + first[i, 0]

    def spread(i):
        second_copy(i).wait_recv()
        parts = pack(field[i, 0, 0, 0] + second[i, 0], field[i, 0, 0, 1] + second[i, 1])
        for g in range(4):
            send_a[4 * i + flip_bits(group, g, 2)] = parts[g]
        for g in range(4):
            if i == 0 and g == 0:
                recv_a[0] = send_a[0]
            else:
                spread_copy(4 * i + g).start()

    for i in ORDER[:AHEAD]:
        start_first(i)
    part_factors()
    edge_factors(0)
    edge_factors(1)
    for n in range(8 + LAG):
        if n < 8:
            start_second(ORDER[n])
        if n + AHEAD < 8:
            start_first(ORDER[n + AHEAD])
        if n >= LAG:
            spread(ORDER[n - LAG])
        if n == 0:
            edge_factors(2)
        elif n < 4:
            level_factors(n - 1)
        elif n == 4:
            small_factors()
    last_copy.wait()
    last_factors()

    pltpu.make_async_remote_copy(
        send_a.at[pl.ds(1, 31)], recv_a.at[pl.ds(1, 31)], a_send, a_recv,
        device_id=partner_x, device_id_type=MESH,
    ).wait_recv()

    def mapped(re, im):
        return jnp.dot(maps[...], split_rows(re, im), preferred_element_type=F32)

    def add_turned(total, values, l, place):
        for c in range(4):
            cos, sin = factor[l, place(c), :K], factor[l, place(c), K:]
            re, im = turn(values[c * K:(c + 1) * K, :LANES], values[c * K:(c + 1) * K, LANES:], cos, sin)
            total[c] = (re, im) if total[c] is None else (total[c][0] + re, total[c][1] + im)

    def finish(re, im, l):
        return turn(re, im, q_cos[l], q_sin[l])

    @pl.loop(0, 2, unroll=True)
    def _(c2):
        total = [None] * 4
        for s1 in range(2):
            for s3 in range(2):
                messages = []
                for s0 in range(2):
                    for t1 in range(2):
                        place = 4 * flip(y2, c2) + 2 * flip(y1, t1) + flip(x0, s0)
                        messages.append(recv_a[4 * place + 2 * flip(x1, s1) + flip(y3, s3)])
                re, im = finish(*unpack(messages), 0)
                add_turned(
                    total, mapped(re, im), 0,
                    lambda c: (c // 2 * 2 + s1) * 8 + c % 2 * 4 + s3 * 2 + c2,
                )
        for c in range(4):
            re, im = finish(*total[c], 1)
            state[0, 2 * c + c2, 0] = re
            state[0, 2 * c + c2, 1] = im

    @pl.loop(0, 4, unroll=2)
    def _(c):
        total = [None] * 4
        for s2 in range(2):
            add_turned(
                total, mapped(state[0, 2 * c + s2, 0], state[0, 2 * c + s2, 1]), 1,
                lambda d: (c // 2 * 2 + d // 2) * 8 + c % 2 * 4 + d % 2 * 2 + s2,
            )
        low = lane_bit((K, LANES), 64)
        for d3 in range(2):
            re, im = finish(*(
                jnp.where(low, a + pltpu.roll(a, 64, 1), b + pltpu.roll(b, 64, 1))
                for a, b in zip(total[d3], total[2 + d3])
            ), 2)
            state[1, 2 * c + d3, 0] = re
            state[1, 2 * c + d3, 1] = im

    def gather_copy(slot):
        return pltpu.make_async_remote_copy(
            send_b.at[slot], recv_b.at[slot // 4, slot % 4], b_send, b_recv.at[slot // 4],
            device_id=gather_device(slot), device_id_type=MESH,
        )

    for r4 in range(2):
        for r3 in range(2):
            d4, d3 = flip(y4, r4), flip(y3, r3)
            total = [None] * 4
            for s in range(2):
                n = 4 * s + 2 * d4 + d3
                add_turned(
                    total, mapped(state[1, n, 0], state[1, n, 1]), 2,
                    lambda c: (s * 2 + c // 2) * 8 + 4 * d4 + 2 * d3 + c % 2,
                )
            low = lane_bit((K, LANES), 32)
            for c2 in range(2):
                re, im = finish(*(
                    jnp.where(low, a + pltpu.roll(a, 96, 1), b + pltpu.roll(b, 32, 1))
                    for a, b in zip(total[c2], total[2 + c2])
                ), 3)
                parts = pack(re, im)
                for e1 in range(2):
                    for e0 in range(2):
                        slot = 16 * r4 + 8 * flip(x0, e0) + 4 * flip(y2, c2) + 2 * flip(x1, e1) + r3
                        send_b[slot] = parts[2 * e1 + e0]
            for slot in range(32):
                if slot // 16 == r4 and slot % 2 == r3:
                    if slot == 0:
                        recv_b[0, 0] = send_b[0]
                    else:
                        gather_copy(slot).start()

    def z_copy(i):
        return pltpu.make_async_remote_copy(
            recv_b.at[i], recv_z.at[i], z_send, z_recv.at[i],
            device_id=partner_z, device_id_type=MESH,
        )

    def x_copy(i):
        return pltpu.make_async_remote_copy(
            recv_b.at[i] if i < 8 else recv_z.at[i - 8], recv_x.at[i], x_send, x_recv.at[i],
            device_id=partner_x, device_id_type=MESH,
        )

    def result_copy(block):
        return pltpu.make_async_copy(staged.at[block], out.at[:, :, block, :], out_sem)

    def expand(*blocks):
        places, parents = [], []
        for fx, fz, i in blocks:
            source = recv_x.at[8 * fz + i] if fx else recv_z.at[i] if fz else recv_b.at[i]
            places.append(
                16 * flip(x2, fx) + 8 * flip(y4, i // 4) + 4 * flip(y2, i % 2)
                + 2 * flip(flip(y1, fz), i % 2) + flip(x0, i // 2 % 2)
            )
            parents.append(split_rows(*unpack([source[flip_bits(group, g, 2)] for g in range(4)])))
        values = jnp.dot(own_map[...], jnp.concatenate(parents, 1), preferred_element_type=F32)
        for n, block in enumerate(places):
            re, im = (values[:, (2 * n + c) * LANES:(2 * n + c + 1) * LANES] for c in range(2))
            staged[block, 0], staged[block, 1] = turn(re, im, last[block, 0], last[block, 1])
            result_copy(block).start()

    def pair(fx, fz, n):
        expand(*((fx, fz, i) for i in GATHER_ORDER[n - 1:n + 1]))

    for n in range(8 + BEHIND):
        if n < 8:
            i = GATHER_ORDER[n]
            arrived = recv_b.at[0, pl.ds(1, 3)] if i == 0 else recv_b.at[i]
            pltpu.make_async_remote_copy(
                arrived, arrived, b_send, b_recv.at[i], device_id=partner_x, device_id_type=MESH
            ).wait_recv()
            z_copy(i).start()
            x_copy(i).start()
            if n % 2:
                pair(0, 0, n)
        m = n - BEHIND
        if m >= 0:
            z_copy(GATHER_ORDER[m]).wait_recv()
            x_copy(8 + GATHER_ORDER[m]).start()
            if m % 2:
                pair(0, 1, m)
    for n in range(1, 8, 2):
        for i in GATHER_ORDER[n - 1:n + 1]:
            x_copy(i).wait_recv()
        pair(1, 0, n)
    for n in range(1, 8, 2):
        for i in GATHER_ORDER[n - 1:n + 1]:
            x_copy(8 + i).wait_recv()
        pair(1, 1, n)

    for sent, sem in (
        (first, first_send), (second, second_send), (send_a.at[pl.ds(1, 31)], a_send),
        (send_b.at[pl.ds(1, 31)], b_send), (recv_z, z_send), (recv_x, x_send),
    ):
        pltpu.make_async_remote_copy(
            sent, sent, sem, a_recv, device_id=partner_x, device_id_type=MESH
        ).wait_send()
    pltpu.make_async_copy(staged, staged, out_sem).wait()


def per_device(coeff, phase_x, phase_y, phase_q, interp):
    field = (2, K, LANES)
    message = (32, LANES)
    dma = pltpu.SemaphoreType.DMA
    result = pl.pallas_call(
        kernel,
        out_shape=jax.ShapeDtypeStruct((2, K, 32, LANES), F32),
        in_specs=[
            pl.BlockSpec(memory_space=pltpu.HBM),
            pl.BlockSpec(memory_space=pltpu.HBM),
            pl.BlockSpec(memory_space=pltpu.HBM),
            pl.BlockSpec(memory_space=pltpu.HBM),
            pl.BlockSpec(memory_space=pltpu.HBM),
        ],
        out_specs=pl.BlockSpec(memory_space=pltpu.VMEM),
        scratch_shapes=[
            pltpu.VMEM((4, 2, 8, K), F32),
            pltpu.VMEM((4, 2, 32, K), F32),
            pltpu.VMEM((4, K, K), F32),
            pltpu.VMEM((8, 2, 2, *field), F32),
            pltpu.VMEM((8, 2, *field), F32),
            pltpu.VMEM((8, *field), F32),
            pltpu.VMEM((32, *message), F32),
            pltpu.VMEM((32, *message), F32),
            pltpu.VMEM((32, *message), F32),
            pltpu.VMEM((8, 4, *message), F32),
            pltpu.VMEM((8, 4, *message), F32),
            pltpu.VMEM((16, 4, *message), F32),
            pltpu.VMEM((2, 8, *field), F32),
            pltpu.VMEM((3, 4, LANES, LANES), F32),
            pltpu.VMEM((3, 8, LANES, LANES), F32),
            pltpu.VMEM((3, 32, LANES, LANES), F32),
            pltpu.VMEM((3, 8, K), F32),
            pltpu.VMEM((3, 8, K), F32),
            pltpu.VMEM((3, 32, K), F32),
            pltpu.VMEM((3, 32, K), F32),
            pltpu.VMEM((4, 2, K, LANES), F32),
            pltpu.VMEM((4, K, LANES), F32),
            pltpu.VMEM((4, K, LANES), F32),
            pltpu.VMEM((32, *field), F32),
            pltpu.VMEM((K, 32 * LANES), F32),
            pltpu.VMEM((32, *field), F32),
            pltpu.VMEM((4 * K, 3 * K), BF16),
            pltpu.VMEM((K, 3 * K), BF16),
            dma((3,)), dma((8,)), dma((2,)), dma, dma((8,)), dma, dma((8,)),
            dma, dma, dma, dma((8,)), dma, dma((8,)), dma, dma((16,)), dma,
        ],
        compiler_params=pltpu.CompilerParams(
            collective_id=0, has_side_effects=True, vmem_limit_bytes=60 * 1024 * 1024
        ),
    )(
        coeff.reshape(2, K, 32, LANES),
        phase_x.transpose(0, 1, 3, 2),
        phase_y.transpose(0, 1, 3, 2),
        phase_q,
        interp,
    )
    return result.reshape(2, K, 1, 1, 32 * LANES)


def solution(mesh):
    placed = (P(None, None, "gx", "gy", None), P(), P(), P(), P())
    return jax.shard_map(
        per_device,
        mesh=mesh,
        in_specs=placed,
        out_specs=P(None, None, "gx", "gy", None),
        check_vma=False,
    )
```

time: 93.4 us -> 76.7 us (0.82); the launches traced: 92.1 us -> 76.5 us
  Pallas kernels: 86.6 us -> 73.4 us
  local copies, waits for them, and re-layouts: 5.48 us -> 3.08 us
    pallas_call x1, Pallas kernels: 86.6 us -> 73.4 us  [per_device(): pl.pallas_call(kernel, out_shape=jax.ShapeDtypeStruct((2, K, 32, LANES),...]
    unnamed x9 -> x1, local copies, waits for them, and re-layouts: 5.48 us -> 3.08 us
where the time goes in v2:
time: 76.7 us; the launch traced here: 76.5 us
  Pallas kernels  73.4 us (96%)
  local copies, waits for them, and re-layouts  3.08 us (4%)
    pallas_call x1, Pallas kernels, per_device(): pl.pallas_call(kernel, out_shape=jax.ShapeDtypeStruct((2, K, 32, LANES),...  73.4 us
    unnamed x1, local copies, waits for them, and re-layouts  3.08 us

profile of v2, /device:TPU:8, one launch (start us, length us, event | category | flops | bytes accessed | tf_op | source)
XLA Modules:
  0.0 76.5 jit_solution(7144368136590566316)
XLA Ops:
  0.0 73.4 %shard_map.55 = f32[2,64,32,128]{3,2,1,0:T(8,128)} custom-call(f32[2,64,32,128]{3,2,1,0:T(8,128)} %bitcast.5, f32[4,2,8,64]{3,2,1,0:T(8,128)} %bitcast.7, f32[4,2,32,64]{3,2,1,0:T(8,128)} %bitcast.6, f32[4,2,64,4096]{3,2,1,0:T(8,128)} %phase_q.1, f32[4,64,64]{2,1,0:T(8,128)} %interp_hbm.1), custom_call_target="tpu_custom_call" | custom-call | tf_op jit(solution)/shard_map/pallas_call | solution.py:459
  73.5 3.1 %copy.8 = f32[2,64,1,1,4096]{4,3,2,1,0:T(1,128)} copy(f32[2,64,1,1,4096]{4,3,2,1,0:T(1,128)} %bitcast.4) | data formatting | bytes 4194304

commit v3 on v2

--- a/solution.py
+++ b/solution.py
@@ -11,11 +11,11 @@
 BF16 = jnp.bfloat16
 K = 64
 LANES = 128
-ORDER = (4, 5, 6, 2, 3, 7, 1, 0)
+ORDER = (4, 5, 6, 7, 2, 3, 1, 0)
 AHEAD = 4
 LAG = 3
 BEHIND = 3
-GATHER_ORDER = (0, 4, 2, 6, 3, 7, 1, 5)
+GATHER_ORDER = (0, 2, 3, 1, 4, 6, 7, 5)
 
 
 def flip(bit, other):
@@ -90,9 +90,9 @@
 
 
 def kernel(
-    coeff, x_hbm, y_hbm, phase_q, interp_hbm, out,
+    coeff, small, phase_q, out,
     phase_x, phase_y, interp, field, first, second, send_a, recv_a, send_b, recv_b, recv_z, recv_x,
-    state, factor_x, factor_y, factor, x_cos, x_sin, y_cos, y_sin, q_own, q_cos, q_sin, last, q_last, staged,
+    partial, state, factor_x, factor_y, factor, x_cos, x_sin, y_cos, y_sin, q_own, q_cos, q_sin, last, q_last, staged,
     maps, own_map,
     small_sem, field_sem, q_sem, first_send, first_recv, second_send, second_recv,
     a_send, a_recv, b_send, b_recv, z_send, z_recv, x_send, x_recv, out_sem,
@@ -121,6 +121,11 @@
         )
 
     barrier = pltpu.get_barrier_semaphore()
+    for slot in range(1, 32):
+        pl.semaphore_signal(barrier, inc=1, device_id=spread_device(slot), device_id_type=MESH)
+    for slot in range(16, 32):
+        pl.semaphore_signal(barrier, inc=1, device_id=gather_device(slot), device_id_type=MESH)
+    pl.semaphore_signal(barrier, inc=1, device_id=device(fx2=1), device_id_type=MESH)
 
     def load(i):
         for fx in range(2):
@@ -131,9 +136,9 @@
                 )
 
     small_copies = [
-        pltpu.make_async_copy(source, target, small_sem.at[n])
-        for n, (source, target) in enumerate(
-            ((x_hbm, phase_x), (y_hbm, phase_y), (interp_hbm, interp))
+        pltpu.make_async_copy(small.at[:, :, pl.ds(first_row, rows), :], target, small_sem.at[n])
+        for n, (first_row, rows, target) in enumerate(
+            ((0, 8, phase_x), (8, 32, phase_y), (40, 32, interp))
         )
     ]
     for copy in small_copies:
@@ -141,11 +146,6 @@
     for i in ORDER:
         for copy in load(i):
             copy.start()
-    for slot in range(1, 32):
-        pl.semaphore_signal(barrier, inc=1, device_id=spread_device(slot), device_id_type=MESH)
-    for slot in range(16, 32):
-        pl.semaphore_signal(barrier, inc=1, device_id=gather_device(slot), device_id_type=MESH)
-    pl.semaphore_signal(barrier, inc=1, device_id=device(fx2=1), device_id_type=MESH)
     own_block = 16 * x2 + 8 * y4 + z
     own_copy = pltpu.make_async_copy(
         phase_q.at[:, :, :, pl.ds(pl.multiple_of(own_block * LANES, LANES), LANES)], q_own, q_sem.at[0]
@@ -174,17 +174,17 @@
     x_first = [ORDER.index(i) % 2 == 0 for i in range(8)]
     partner_x, partner_y, partner_z = device(fx2=1), device(fy4=1), device(fy1=1)
 
-    def first_copy(i):
+    def first_copy(i, c):
         return pltpu.make_async_remote_copy(
-            field.at[i, 1] if x_first[i] else field.at[i, :, 1],
-            first.at[i], first_send, first_recv.at[i],
+            field.at[i, 1, :, c] if x_first[i] else field.at[i, :, 1, c],
+            first.at[i, :, c], first_send, first_recv.at[i, c],
             device_id=partner_x if x_first[i] else partner_y, device_id_type=MESH,
         )
 
-    def second_copy(i):
+    def second_copy(i, c):
         return pltpu.make_async_remote_copy(
-            field.at[i, 0, 1] if x_first[i] else field.at[i, 1, 0],
-            second.at[i], second_send, second_recv.at[i],
+            field.at[i, 0, 1, c] if x_first[i] else field.at[i, 1, 0, c],
+            second.at[i, c], second_send, second_recv.at[i, c],
             device_id=partner_y if x_first[i] else partner_x, device_id_type=MESH,
         )
 
@@ -224,6 +224,9 @@
             factor[l, n, :K] = cos
             factor[l, n, K:] = sin
 
+    def block_of(c):
+        return jnp.concatenate([interp[c, 0], interp[c, 1]], 0)
+
     def small_factors():
         own_copy.wait()
         for l in range(4):
@@ -233,8 +236,8 @@
             value = value + pltpu.roll(value, 32, 1)
             value = value + pltpu.roll(value, 64, 1)
             q_cos[l], q_sin[l] = cos_sin(value)
-        maps[...] = jnp.concatenate([split_columns(interp[c]) for c in range(4)], 0)
-        own_map[...] = split_columns(interp[2 * x2 + y1])
+        maps[...] = jnp.concatenate([split_columns(block_of(c)) for c in range(4)], 0)
+        own_map[...] = split_columns(block_of(2 * x2 + y1))
 
     def last_factors():
         @pl.loop(0, 32, unroll=4)
@@ -246,25 +249,28 @@
         pltpu.make_async_copy(field.at[i], field.at[i], field_sem.at[i]).wait()
         for fx, fy in ((1, 1), (1, 0) if x_first[i] else (0, 1)):
             rotate(i, fx, fy)
-        first_copy(i).start()
+        first_copy(i, 0).start()
+        first_copy(i, 1).start()
         for fx, fy in ((0, 0), (0, 1) if x_first[i] else (1, 0)):
             rotate(i, fx, fy)
 
     def spread_copy(slot):
         return pltpu.make_async_remote_copy(
-            send_a.at[slot], recv_a.at[slot], a_send, a_recv,
+            send_a.at[slot], recv_a.at[slot], a_send, a_recv.at[slot // 16],
             device_id=spread_device(slot), device_id_type=MESH,
         )
 
     def start_second(i):
-        first_copy(i).wait_recv()
         fx, fy = (0, 1) if x_first[i] else (1, 0)
-        field[i, fx, fy] = field[i, fx, fy] + first[i, 1]
-        second_copy(i).start()
+        for c in range(2):
+            first_copy(i, c).wait_recv()
+            field[i, fx, fy, c] = field[i, fx, fy, c] + first[i, 1, c]
+            second_copy(i, c).start()
         field[i, 0, 0] = field[i, 0, 0] + first[i, 0]
 
     def spread(i):
-        second_copy(i).wait_recv()
+        second_copy(i, 0).wait_recv()
+        second_copy(i, 1).wait_recv()
         parts = pack(field[i, 0, 0, 0] + second[i, 0], field[i, 0, 0, 1] + second[i, 1])
         for g in range(4):
             send_a[4 * i + flip_bits(group, g, 2)] = parts[g]
@@ -276,6 +282,8 @@
 
     for i in ORDER[:AHEAD]:
         start_first(i)
+    last_copy.wait()
+    last_factors()
     part_factors()
     edge_factors(0)
     edge_factors(1)
@@ -292,13 +300,6 @@
             level_factors(n - 1)
         elif n == 4:
             small_factors()
-    last_copy.wait()
-    last_factors()
-
-    pltpu.make_async_remote_copy(
-        send_a.at[pl.ds(1, 31)], recv_a.at[pl.ds(1, 31)], a_send, a_recv,
-        device_id=partner_x, device_id_type=MESH,
-    ).wait_recv()
 
     def mapped(re, im):
         return jnp.dot(maps[...], split_rows(re, im), preferred_element_type=F32)
@@ -312,15 +313,20 @@
     def finish(re, im, l):
         return turn(re, im, q_cos[l], q_sin[l])
 
-    @pl.loop(0, 2, unroll=True)
-    def _(c2):
+    low = lane_bit((K, LANES), 64)
+    for r2 in (1, 0):
+        arrived = recv_a.at[pl.ds(16, 16)] if r2 else recv_a.at[pl.ds(1, 15)]
+        pltpu.make_async_remote_copy(
+            arrived, arrived, a_send, a_recv.at[r2], device_id=partner_x, device_id_type=MESH
+        ).wait_recv()
+        c2 = flip(y2, r2)
         total = [None] * 4
         for s1 in range(2):
             for s3 in range(2):
                 messages = []
                 for s0 in range(2):
                     for t1 in range(2):
-                        place = 4 * flip(y2, c2) + 2 * flip(y1, t1) + flip(x0, s0)
+                        place = 4 * r2 + 2 * flip(y1, t1) + flip(x0, s0)
                         messages.append(recv_a[4 * place + 2 * flip(x1, s1) + flip(y3, s3)])
                 re, im = finish(*unpack(messages), 0)
                 add_turned(
@@ -328,26 +334,23 @@
                     lambda c: (c // 2 * 2 + s1) * 8 + c % 2 * 4 + s3 * 2 + c2,
                 )
         for c in range(4):
-            re, im = finish(*total[c], 1)
-            state[0, 2 * c + c2, 0] = re
-            state[0, 2 * c + c2, 1] = im
-
-    @pl.loop(0, 4, unroll=2)
-    def _(c):
-        total = [None] * 4
-        for s2 in range(2):
+            parent = finish(*total[c], 1)
+            children = [None] * 4
+            if r2 == 0:
+                children = [(partial[c, d, 0], partial[c, d, 1]) for d in range(4)]
             add_turned(
-                total, mapped(state[0, 2 * c + s2, 0], state[0, 2 * c + s2, 1]), 1,
-                lambda d: (c // 2 * 2 + d // 2) * 8 + c % 2 * 4 + d % 2 * 2 + s2,
+                children, mapped(*parent), 1,
+                lambda d: (c // 2 * 2 + d // 2) * 8 + c % 2 * 4 + d % 2 * 2 + c2,
             )
-        low = lane_bit((K, LANES), 64)
-        for d3 in range(2):
-            re, im = finish(*(
-                jnp.where(low, a + pltpu.roll(a, 64, 1), b + pltpu.roll(b, 64, 1))
-                for a, b in zip(total[d3], total[2 + d3])
-            ), 2)
-            state[1, 2 * c + d3, 0] = re
-            state[1, 2 * c + d3, 1] = im
+            if r2 == 1:
+                for d in range(4):
+                    partial[c, d, 0], partial[c, d, 1] = children[d]
+                continue
+            for d3 in range(2):
+                state[2 * c + d3, 0], state[2 * c + d3, 1] = finish(*(
+                    jnp.where(low, a + pltpu.roll(a, 64, 1), b + pltpu.roll(b, 64, 1))
+                    for a, b in zip(children[d3], children[2 + d3])
+                ), 2)
 
     def gather_copy(slot):
         return pltpu.make_async_remote_copy(
@@ -362,7 +365,7 @@
             for s in range(2):
                 n = 4 * s + 2 * d4 + d3
                 add_turned(
-                    total, mapped(state[1, n, 0], state[1, n, 1]), 2,
+                    total, mapped(state[n, 0], state[n, 1]), 2,
                     lambda c: (s * 2 + c // 2) * 8 + 4 * d4 + 2 * d3 + c % 2,
                 )
             low = lane_bit((K, LANES), 32)
@@ -447,7 +450,7 @@
         (send_b.at[pl.ds(1, 31)], b_send), (recv_z, z_send), (recv_x, x_send),
     ):
         pltpu.make_async_remote_copy(
-            sent, sent, sem, a_recv, device_id=partner_x, device_id_type=MESH
+            sent, sent, sem, a_recv.at[0], device_id=partner_x, device_id_type=MESH
         ).wait_send()
     pltpu.make_async_copy(staged, staged, out_sem).wait()
 
@@ -460,17 +463,15 @@
         kernel,
         out_shape=jax.ShapeDtypeStruct((2, K, 32, LANES), F32),
         in_specs=[
-            pl.BlockSpec(memory_space=pltpu.HBM),
-            pl.BlockSpec(memory_space=pltpu.HBM),
-            pl.BlockSpec(memory_space=pltpu.HBM),
-            pl.BlockSpec(memory_space=pltpu.HBM),
-            pl.BlockSpec(memory_space=pltpu.HBM),
+            pl.BlockSpec(memory_space=pl.ANY),
+            pl.BlockSpec(memory_space=pl.ANY),
+            pl.BlockSpec(memory_space=pl.ANY),
         ],
         out_specs=pl.BlockSpec(memory_space=pltpu.VMEM),
         scratch_shapes=[
             pltpu.VMEM((4, 2, 8, K), F32),
             pltpu.VMEM((4, 2, 32, K), F32),
-            pltpu.VMEM((4, K, K), F32),
+            pltpu.VMEM((4, 2, 32, K), F32),
             pltpu.VMEM((8, 2, 2, *field), F32),
             pltpu.VMEM((8, 2, *field), F32),
             pltpu.VMEM((8, *field), F32),
@@ -480,7 +481,8 @@
             pltpu.VMEM((8, 4, *message), F32),
             pltpu.VMEM((8, 4, *message), F32),
             pltpu.VMEM((16, 4, *message), F32),
-            pltpu.VMEM((2, 8, *field), F32),
+            pltpu.VMEM((4, 4, *field), F32),
+            pltpu.VMEM((8, *field), F32),
             pltpu.VMEM((3, 4, LANES, LANES), F32),
             pltpu.VMEM((3, 8, LANES, LANES), F32),
             pltpu.VMEM((3, 32, LANES, LANES), F32),
@@ -496,18 +498,18 @@
             pltpu.VMEM((32, *field), F32),
             pltpu.VMEM((4 * K, 3 * K), BF16),
             pltpu.VMEM((K, 3 * K), BF16),
-            dma((3,)), dma((8,)), dma((2,)), dma, dma((8,)), dma, dma((8,)),
-            dma, dma, dma, dma((8,)), dma, dma((8,)), dma, dma((16,)), dma,
+            dma((3,)), dma((8,)), dma((2,)), dma, dma((8, 2)), dma, dma((8, 2)),
+            dma, dma((2,)), dma, dma((8,)), dma, dma((8,)), dma, dma((16,)), dma,
         ],
         compiler_params=pltpu.CompilerParams(
-            collective_id=0, has_side_effects=True, vmem_limit_bytes=60 * 1024 * 1024
+            collective_id=0, has_side_effects=True, vmem_limit_bytes=51 * 1024 * 1024
         ),
     )(
         coeff.reshape(2, K, 32, LANES),
-        phase_x.transpose(0, 1, 3, 2),
-        phase_y.transpose(0, 1, 3, 2),
+        jnp.concatenate(
+            [phase_x.transpose(0, 1, 3, 2), phase_y.transpose(0, 1, 3, 2), interp.reshape(4, 2, 32, K)], 2
+        ),
         phase_q,
-        interp,
     )
     return result.reshape(2, K, 1, 1, 32 * LANES)
 

time: 76.7 us -> 73 us (0.952)
  Pallas kernels: 73.4 us -> 70.6 us
  local copies, waits for them, and re-layouts: 3.08 us -> 1.32 us
  other arithmetic: 0 us -> 0.99 us
    pallas_call x1, Pallas kernels: 73.4 us -> 70.6 us  [per_device(): pl.pallas_call(kernel, out_shape=jax.ShapeDtypeStruct((2, K, 32, LANES),...]
    unnamed x1, local copies, waits for them, and re-layouts: 3.08 us -> 1.32 us
    concatenate x0 -> x1, other arithmetic: none -> 0.99 us  [per_device(): jnp.concatenate([phase_x.transpose(0, 1, 3, 2), phase_y.transpose(0, 1, 3...]
where the time goes in v3:
time: 73 us; the launch traced here: 72.9 us
  Pallas kernels  70.6 us (97%)
  local copies, waits for them, and re-layouts  1.32 us (2%)
  other arithmetic  0.99 us (1%)
    pallas_call x1, Pallas kernels, per_device(): pl.pallas_call(kernel, out_shape=jax.ShapeDtypeStruct((2, K, 32, LANES),...  70.6 us

profile of v3, /device:TPU:8, one launch (start us, length us, event | category | flops | bytes accessed | tf_op | source)
XLA Modules:
  0.0 72.9 jit_solution(6770375556375849795)
XLA Ops:
  0.0 1.0 %pad_maximum_fusion.small = f32[4,2,72,64]{3,2,1,0:T(8,128)S(1)} fusion(f32[4,2,32,64]{3,2,1,0:T(8,128)} %bitcast.7, f32[4,2,32,64]{3,2,1,0:T(8,128)} %bitcast.8, f32[4,2,8,64]{3,2,1,0:T(8,128)} %bitcast.9), kind=kLoop, calls=%fused_computation | loop fusion | flops 73728 | bytes 294912 | tf_op jit(solution)/shard_map/concatenate | solution.py:509
  1.0 70.6 %shard_map.55 = f32[2,64,32,128]{3,2,1,0:T(8,128)S(1)} custom-call(f32[2,64,32,128]{3,2,1,0:T(8,128)} %bitcast.6, f32[4,2,72,64]{3,2,1,0:T(8,128)S(1)} %pad_maximum_fusion.small, f32[4,2,64,4096]{3,2,1,0:T(8,128)} %phase_q.1), custom_call_target="tpu_custom_call" | custom-call | tf_op jit(solution)/shard_map/pallas_call | solution.py:462
  71.6 1.3 %copy.8 = f32[2,64,1,1,4096]{4,3,2,1,0:T(1,128)} copy(f32[2,64,1,1,4096]{4,3,2,1,0:T(1,128)S(1)} %bitcast.5) | data formatting | bytes 4194304

commit v4 on v3

--- a/solution.py
+++ b/solution.py
@@ -11,7 +11,7 @@
 BF16 = jnp.bfloat16
 K = 64
 LANES = 128
-ORDER = (4, 5, 6, 7, 2, 3, 1, 0)
+ORDER = (4, 5, 6, 7, 3, 2, 1, 0)
 AHEAD = 4
 LAG = 3
 BEHIND = 3

time: 73 us -> 73.5 us (level)
  no operation moved by 1% of the time
where the time goes in v4:
time: 73.5 us; the launch traced here: 73.4 us
  Pallas kernels  71.1 us (97%)
  local copies, waits for them, and re-layouts  1.32 us (2%)
  other arithmetic  0.99 us (1%)
    pallas_call x1, Pallas kernels, per_device(): pl.pallas_call(kernel, out_shape=jax.ShapeDtypeStruct((2, K, 32, LANES),...  71.1 us

profile of v4, /device:TPU:8, one launch (start us, length us, event | category | flops | bytes accessed | tf_op | source)
XLA Modules:
  0.0 73.4 jit_solution(12652748991797077262)
XLA Ops:
  0.0 1.0 %pad_maximum_fusion.small = f32[4,2,72,64]{3,2,1,0:T(8,128)S(1)} fusion(f32[4,2,32,64]{3,2,1,0:T(8,128)} %bitcast.7, f32[4,2,32,64]{3,2,1,0:T(8,128)} %bitcast.8, f32[4,2,8,64]{3,2,1,0:T(8,128)} %bitcast.9), kind=kLoop, calls=%fused_computation | loop fusion | flops 73728 | bytes 294912 | tf_op jit(solution)/shard_map/concatenate | solution.py:509
  1.0 71.1 %shard_map.55 = f32[2,64,32,128]{3,2,1,0:T(8,128)S(1)} custom-call(f32[2,64,32,128]{3,2,1,0:T(8,128)} %bitcast.6, f32[4,2,72,64]{3,2,1,0:T(8,128)S(1)} %pad_maximum_fusion.small, f32[4,2,64,4096]{3,2,1,0:T(8,128)} %phase_q.1), custom_call_target="tpu_custom_call" | custom-call | tf_op jit(solution)/shard_map/pallas_call | solution.py:462
  72.1 1.3 %copy.8 = f32[2,64,1,1,4096]{4,3,2,1,0:T(1,128)} copy(f32[2,64,1,1,4096]{4,3,2,1,0:T(1,128)S(1)} %bitcast.5) | data formatting | bytes 4194304
